TPU v7x, 32 devices: a whole 2x2x4 slice. The times are simulated.
32 devices in a mesh: gx: 8 (over z, core), gy: 4 (over y, x).
Axes of the slice: x: 2, y: 2, z: 4, core: 2. Of those that a mesh axis runs over, the one named last changes fastest.
Arguments:
- u_field: float32 [256, 1024], P('gx', 'gy'), may hold values from -6 to 6
- v_field: float32 [256, 1024], P('gx', 'gy'), may hold values from -6 to 6
- w_first: bfloat16 [9, 64, 2], replicated, may hold values from -1.5 to 1.5
- b_first: float32 [64], replicated, may hold values from -3 to 3
- w_second: bfloat16 [9, 64, 64], replicated, may hold values from -0.25 to 0.25
- b_second: float32 [64], replicated, may hold values from -3 to 3
- w_third: bfloat16 [9, 16, 64], replicated, may hold values from -0.25 to 0.25
- b_third: float32 [16], replicated, may hold values from -3 to 3
Outputs:
- u_next: float32 [256, 1024], P('gx', 'gy')
- v_next: float32 [256, 1024], P('gx', 'gy')
All inputs are finite; a program needn't handle non-finite values.
Results may differ from a plain program's by a relative error of at most 0.0023.
Values sent between devices are 32-bit elements; how exact they have to be, the bound alone decides.
No kernel may reach another device: no remote copies, remote signals or barrier semaphores. Data moves between devices by JAX's collectives and lax.ppermute only.
A program may use at most 64 MiB of HBM per device.

v0:
```python
import math

import jax
import jax.numpy as jnp
from jax import lax
from jax.sharding import PartitionSpec as P

step_ratio = 0.4
stencil_base = (-0.0625, 0.5625, 0.5625, -0.0625)
block_height = 8
highest = lax.Precision.HIGHEST


def padded_2(value, sides, width):
    for axis, dim in sides:
        peers, length = (lax.axis_size(axis), value.shape[dim])
        up = [(i, (i + 1) % peers) for i in range(peers)]
        down = [(j, i) for i, j in up]
        last = lax.slice_in_dim(value, length - width, length, axis=dim)
        first = lax.slice_in_dim(value, 0, width, axis=dim)
        before = lax.ppermute(last, axis, up)
        after = lax.ppermute(first, axis, down)
        value = jnp.concatenate([before, value, after], axis=dim)
    return value


def from_behind(block, axis, distance):
    devices = range(lax.axis_size(axis))
    route = [((i - distance) % len(devices), i) for i in devices]
    return lax.ppermute(block, axis, route)


def convolve(inputs, kernel, offsets, height, breadth):
    summed = None
    for tap_index in range(9):
        shift_down = tap_index // 3
        shift_right = tap_index % 3
        window = inputs[:, shift_down : shift_down + height, shift_right : shift_right + breadth]
        term = jnp.einsum(
            "oc,chw->ohw", kernel[tap_index], window, preferred_element_type=jnp.float32
        )
        summed = term if summed is None else summed + term
    return summed + offsets[:, None, None]


def predict(features, layers, top_row, left_col, height, breadth):
    w_first, b_first, w_second, b_second, w_third, b_third = layers
    inputs = lax.dynamic_slice(
        features, (0, top_row, left_col), (features.shape[0], height + 6, breadth + 6)
    )
    first = jax.nn.relu(convolve(inputs, w_first, b_first, height + 4, breadth + 4)).astype(
        jnp.bfloat16
    )
    second = jax.nn.relu(convolve(first, w_second, b_second, height + 2, breadth + 2)).astype(
        jnp.bfloat16
    )
    return convolve(second, w_third, b_third, height, breadth)


def coefficients(features, layers, margin, first_col, breadth):
    height = features.shape[1] - 2 * margin
    initial = jnp.zeros((layers[4].shape[1], height, breadth), jnp.float32)

    def advance(position, outputs):
        start_row = position * block_height
        piece = predict(
            features, layers, start_row + margin - 3, margin - 3 + first_col, block_height, breadth
        )
        return lax.dynamic_update_slice(outputs, piece, (0, start_row, 0))

    return lax.fori_loop(0, height // block_height, advance, initial)


def fluxes(padded, coeff, margin, anchor, height, breadth):

    def sample(shift_down, shift_right):
        top_row = margin + anchor + shift_down
        left_col = margin + anchor + shift_right
        return padded[:, top_row : top_row + height, left_col : left_col + breadth]

    weights = coeff.reshape(2, 2, 4, height, breadth)
    weights = (
        jnp.asarray(stencil_base, jnp.float32)[:, None, None]
        + weights
        - jnp.mean(weights, axis=2, keepdims=True)
    )
    centre = sample(0, 0)
    east = (
        weights[0, :, 0] * sample(-1, 0)
        + weights[0, :, 1] * centre
        + weights[0, :, 2] * sample(1, 0)
        + weights[0, :, 3] * sample(2, 0)
    )
    north = (
        weights[1, :, 0] * sample(0, -1)
        + weights[1, :, 1] * centre
        + weights[1, :, 2] * sample(0, 1)
        + weights[1, :, 3] * sample(0, 2)
    )
    carry_x = 0.5 * (centre[0] + sample(1, 0)[0])
    carry_y = 0.5 * (centre[1] + sample(0, 1)[1])
    return (carry_x * east, carry_y * north)


def dft_table(length, sign):
    counter = jnp.arange(length, dtype=jnp.int32)
    phases = counter[:, None] * counter[None, :] % length
    phases = phases.astype(jnp.float32) * (sign * 2.0 * math.pi / length)
    return (jnp.cos(phases), jnp.sin(phases))


def rotate(spectra, cosine, sine, form):

    def product(matrix, values):
        return jnp.einsum(form, matrix, values, precision=highest)

    if spectra.shape[0] == 1:
        return jnp.stack([product(cosine, spectra[0]), product(sine, spectra[0])])
    real_part = spectra[0]
    imag_part = spectra[1]
    return jnp.stack(
        [
            product(cosine, real_part) - product(sine, imag_part),
            product(cosine, imag_part) + product(sine, real_part),
        ]
    )


def twiddle(spectra, phases):
    cosine = jnp.cos(phases)
    sine = jnp.sin(phases)
    real_part = spectra[0]
    imag_part = spectra[1]
    return jnp.stack([real_part * cosine - imag_part * sine, real_part * sine + imag_part * cosine])


def row_section(spectra, sign):
    members = lax.axis_size("gx")
    own_index = lax.axis_index("gx")
    length = spectra.shape[2]
    sub_rows = length // members
    whole = members * length
    local_cos, local_sin = dft_table(length, sign)
    if sign > 0:
        spectra = rotate(spectra, local_cos, local_sin, "mp,fpy->fmy")

    def through(pieces):
        group_cos, group_sin = dft_table(members, sign)
        cell_rows = own_index * sub_rows + jnp.arange(sub_rows, dtype=jnp.int32)
        frequency = jnp.arange(members, dtype=jnp.int32)
        phases = (frequency[:, None] * cell_rows[None, :] % whole).astype(jnp.float32) * (
            sign * 2.0 * math.pi / whole
        )
        if sign < 0:
            return twiddle(
                rotate(pieces, group_cos, group_sin, "ka,fasy->fksy"), phases[:, :, None]
            )
        return rotate(twiddle(pieces, phases[:, :, None]), group_cos, group_sin, "ak,fksy->fasy")[
            :1
        ]

    shaped = spectra.reshape(spectra.shape[0], 2, 1, length, spectra.shape[3])
    arrived = lax.all_to_all(shaped, "gx", split_axis=3, concat_axis=2, tiled=True)
    turned = through(arrived)
    returned = lax.all_to_all(turned, "gx", split_axis=2, concat_axis=3, tiled=True)
    returned = returned.reshape(returned.shape[0], 2, returned.shape[3], returned.shape[4])
    if sign < 0:
        returned = rotate(returned, local_cos, local_sin, "pm,fmy->fpy")
    return returned


def column_local(pieces, sign, members):
    length = pieces.shape[4]
    whole = members * length
    group_cos, group_sin = dft_table(members, sign)
    local_cos, local_sin = dft_table(length, sign)
    frequency = jnp.arange(members, dtype=jnp.int32)
    column_ids = jnp.arange(length, dtype=jnp.int32)
    phases = (frequency[:, None] * column_ids[None, :] % whole).astype(jnp.float32) * (
        sign * 2.0 * math.pi / whole
    )
    phases = phases[:, None, :]
    if sign < 0:
        turned = twiddle(rotate(pieces, group_cos, group_sin, "kb,fbpj->fkpj"), phases)
        return rotate(turned, local_cos, local_sin, "qj,fkpj->fkpq")
    turned = twiddle(rotate(pieces, local_cos, local_sin, "jq,fkpq->fkpj"), phases)
    return rotate(turned, group_cos, group_sin, "bk,fkpj->fbpj")


def column_out(spectra, sign):
    members = lax.axis_size("gy")
    shaped = spectra.reshape(2, 2, 1, spectra.shape[2], spectra.shape[3])
    arrived = lax.all_to_all(shaped, "gy", split_axis=3, concat_axis=2, tiled=True)
    return column_local(arrived, sign, members)


def column_home(spectra):
    returned = lax.all_to_all(spectra, "gy", split_axis=2, concat_axis=3, tiled=True)
    return returned.reshape(2, 2, returned.shape[3], returned.shape[4])


def wavenumber(counter, whole):
    signed = jnp.where(counter >= whole // 2, counter - whole, counter)
    return signed.astype(jnp.float32) * (2.0 * math.pi / whole)


def project(spectra, wave_x, wave_y):
    denominator = wave_x * wave_x + wave_y * wave_y
    denominator = jnp.where(denominator > 0, denominator, 1.0)
    shared = (wave_x * spectra[:, 0] + wave_y * spectra[:, 1]) / denominator
    return jnp.stack([spectra[:, 0] - wave_x * shared, spectra[:, 1] - wave_y * shared], axis=1)


def on_device(u_field, v_field, w_first, b_first, w_second, b_second, w_third, b_third):
    field = jnp.stack([u_field, v_field])
    height, breadth = u_field.shape
    layers = (w_first, b_first, w_second, b_second, w_third, b_third)
    padded = padded_2(field, (("gx", 1), ("gy", 2)), 3)
    features = padded.astype(jnp.bfloat16)
    coeff = coefficients(features, layers, 3, 0, breadth)
    east_now, north_now = fluxes(padded, coeff, 3, 0, height, breadth)
    below = from_behind(east_now[:, -1:, :], "gx", 1)
    beside = from_behind(north_now[:, :, -1:], "gy", 1)
    east_before = jnp.concatenate([below, east_now[:, :-1]], axis=1)
    north_before = jnp.concatenate([beside, north_now[:, :, :-1]], axis=2)
    star = field - step_ratio * (east_now - east_before + north_now - north_before)
    grid_x = height * lax.axis_size("gx")
    grid_y = breadth * lax.axis_size("gy")
    index_x = lax.axis_index("gx")
    index_y = lax.axis_index("gy")
    spectra = row_section(star[None], -1)
    spread = column_out(spectra, -1)
    sub_rows = height // lax.axis_size("gy")
    within = jnp.arange(sub_rows, dtype=jnp.int32)
    wave_x = wavenumber(index_x + lax.axis_size("gx") * (index_y * sub_rows + within), grid_x)[
        None, :, None
    ]
    frequency = jnp.arange(lax.axis_size("gy"), dtype=jnp.int32)
    column_ids = jnp.arange(breadth, dtype=jnp.int32)
    wave_y = wavenumber(frequency[:, None] + lax.axis_size("gy") * column_ids[None, :], grid_y)[
        :, None, :
    ]
    spread = project(spread, wave_x, wave_y)
    spectra = column_home(column_local(spread, 1, lax.axis_size("gy")))
    result = row_section(spectra, 1)
    scale = 1.0 / (grid_x * grid_y)
    return (result[0, 0] * scale, result[0, 1] * scale)


def solution(mesh):
    return jax.shard_map(
        on_device,
        mesh=mesh,
        in_specs=(P("gx", "gy"), P("gx", "gy"), P(), P(), P(), P(), P(), P()),
        out_specs=(P("gx", "gy"), P("gx", "gy")),
        check_vma=False,
    )
```

profile of v0, /device:TPU:0, one launch (start us, length us, event | category | flops | bytes accessed | tf_op | source)
XLA Modules:
  0.0 133.5 jit_solution(13580778779274590585)
XLA Ops:
  1.5 4.5 %collective-permute-start = (f32[2,3,256]{2,1,0:T(4,128)S(1)}, f32[2,3,256]{2,1,0:T(4,128)S(1)}, u32[]{:S(2)}, u32[]{:S(2)}) collective-permute-start(f32[2,3,256]{2,1,0:T(4,128)S(1)} %get-tuple-element.348), channel_id=1, source_target_pairs={{4,0},{8,4},{12,8},{16,12},{20,16},{24,20},{28,24},{0,28},{5,1},{9... | collective-permute-start | bytes 18440 | tf_op jit(solution)/shard_map/ppermute | solution.py:22
  6.0 1.3 %collective-permute-done = f32[2,3,256]{2,1,0:T(4,128)S(1)} collective-permute-done((f32[2,3,256]{2,1,0:T(4,128)S(1)}, f32[2,3,256]{2,1,0:T(4,128)S(1)}, u32[]{:S(2)}, u32[]{:S(2)}) %collective-permute-start) | collective-permute-done | bytes 6176 | tf_op jit(solution)/shard_map/ppermute | solution.py:22
  7.4 3.5 %collective-permute-done.1 = f32[2,3,256]{2,1,0:T(4,128)S(1)} collective-permute-done((f32[2,3,256]{2,1,0:T(4,128)S(1)}, f32[2,3,256]{2,1,0:T(4,128)S(1)}, u32[]{:S(2)}, u32[]{:S(2)}) %collective-permute-start.1) | collective-permute-done | bytes 6176 | tf_op jit(solution)/shard_map/ppermute | solution.py:21
  11.8 2.5 %collective-permute-start.3 = (f32[2,38,3]{2,1,0:T(8,128)S(1)}, f32[2,38,3]{2,1,0:T(8,128)S(1)}, u32[]{:S(2)}, u32[]{:S(2)}) collective-permute-start(f32[2,38,3]{2,1,0:T(8,128)S(1)} %get-tuple-element.344), channel_id=1, source_target_pairs={{1,0},{2,1},{3,2},{0,3},{5,4},{6,5},{7,6},{4,7},{9,8},{10,9},{11,1... | collective-permute-start | bytes 2744 | tf_op jit(solution)/shard_map/ppermute | solution.py:22
  16.6 2.5 %collective-permute-done.2 = f32[2,38,3]{2,1,0:T(8,128)S(1)} collective-permute-done((f32[2,38,3]{2,1,0:T(8,128)S(1)}, f32[2,38,3]{2,1,0:T(8,128)S(1)}, u32[]{:S(2)}, u32[]{:S(2)}) %collective-permute-start.2) | collective-permute-done | bytes 944 | tf_op jit(solution)/shard_map/ppermute | solution.py:21
  19.4 34.6 %while.17 = (s32[]{:T(128)}, f32[16,32,256]{2,1,0:T(8,128)S(1)}, bf16[2,38,262]{2,0,1:T(2,128)(2,1)S(1)}, bf16[9,64,2]{1,2,0:T(2,128)(2,1)S(1)}, f32[64]{0:T(128...) while((s32[]{:T(128)}, f32[16,32,256]{2,1,0:T(8,128)S(1)}, ...), condition=%wide.region_1.2_spmd, body=%wide.region_0.1_spmd.sunk | while | flops 239463184 | bytes 39334732 | solution.py:71
  55.3 4.8 %collective-permute-done.5 = f32[2,32,1]{2,1,0:T(8,128)S(1)} collective-permute-done((f32[2,32,1]{2,1,0:T(8,128)S(1)}, f32[2,32,1]{2,1,0:T(8,128)S(1)}, u32[]{:S(2)}, u32[]{:S(2)}) %collective-permute-start.5) | collective-permute-done | bytes 288 | tf_op jit(solution)/shard_map/ppermute | solution.py:30
  60.9 3.7 %all-to-all-start = ((f32[1,2,1,32,256]{4,1,2,0,3:T(2,128)}), f32[1,2,1,32,256]{4,1,2,0,3:T(2,128)S(1)}, u32[]{:S(2)}, u32[]{:S(2)}) async-start(f32[1,2,1,32,256]{4,1,2,0,3:T(2,128)} %copy.170), calls=%async_computation | async-start | bytes 131072 | tf_op jit(solution)/shard_map/all_to_all | solution.py:163
  64.7 5.7 %all-to-all-done = f32[1,2,1,32,256]{4,1,2,0,3:T(2,128)S(1)} async-done(((f32[1,2,1,32,256]{4,1,2,0,3:T(2,128)}), f32[1,2,1,32,256]{4,1,2,0,3:T(2,128)S(1)}, u32[]{:S(2)}, u32[]{:S(2)}) %all-to-all-start) | async-done | bytes 65568 | tf_op jit(solution)/shard_map/all_to_all | solution.py:163
  71.7 3.4 %all-to-all-start.1 = ((f32[2,2,8,4,256]{4,3,1,0,2:T(4,128)}), f32[2,2,8,4,256]{4,3,1,0,2:T(4,128)S(1)}, u32[]{:S(2)}, u32[]{:S(2)}) async-start(f32[2,2,8,4,256]{4,3,1,0,2:T(4,128)} %copy.173), calls=%async_computation.1 | async-start | bytes 262144 | tf_op jit(solution)/shard_map/all_to_all | solution.py:165
  75.1 6.6 %all-to-all-done.1 = f32[2,2,8,4,256]{4,3,1,0,2:T(4,128)S(1)} async-done(((f32[2,2,8,4,256]{4,3,1,0,2:T(4,128)}), f32[2,2,8,4,256]{4,3,1,0,2:T(4,128)S(1)}, u32[]{:S(2)}, u32[]{:S(2)}) %all-to-all-start.1) | async-done | bytes 131104 | tf_op jit(solution)/shard_map/all_to_all | solution.py:165
  83.7 3.5 %all-to-all-start.2 = ((f32[2,2,1,32,256]{4,1,0,2,3:T(2,128)}), f32[2,2,1,32,256]{4,1,0,2,3:T(2,128)S(1)}, u32[]{:S(2)}, u32[]{:S(2)}) async-start(f32[2,2,1,32,256]{4,1,0,2,3:T(2,128)} %copy.180), calls=%async_computation.2 | async-start | bytes 262144 | tf_op jit(solution)/shard_map/all_to_all | solution.py:193
  87.3 4.7 %all-to-all-done.2 = f32[2,2,1,32,256]{4,1,0,2,3:T(2,128)S(1)} async-done(((f32[2,2,1,32,256]{4,1,0,2,3:T(2,128)}), f32[2,2,1,32,256]{4,1,0,2,3:T(2,128)S(1)}, u32[]{:S(2)}, u32[]{:S(2)}) %all-to-all-start.2) | async-done | bytes 131104 | tf_op jit(solution)/shard_map/all_to_all | solution.py:193
  93.3 1.3 fusion.126
  94.6 1.3 fusion.124
  95.9 1.3 fusion.113
  97.3 1.3 fusion.112
  98.7 1.3 fusion.118
  100.0 1.3 fusion.120
  101.3 1.3 convolution_subtract_fusion.5
  102.6 1.3 multiply_subtract_fusion
  105.3 7.4 %all_to_all.24 = f32[2,2,4,8,256]{4,3,1,0,2:T(8,128)S(1)} all-to-all(f32[2,2,4,8,256]{4,3,1,0,2:T(8,128)S(1)} %copy.195), channel_id=1, replica_groups=mesh['gx'=8,'gy'=4] {'gy'}, dimensions={2} | all-to-all | bytes 262144 | tf_op jit(solution)/shard_map/all_to_all | solution.py:198
  113.9 9.2 %all_to_all.25 = f32[2,2,1,32,256]{4,1,0,2,3:T(2,128)S(1)} all-to-all(f32[2,2,1,32,256]{4,1,0,2,3:T(2,128)S(1)} %copy.198), channel_id=1, replica_groups=mesh['gx'=8,'gy'=4] {'gx'}, dimensions={3} | all-to-all | bytes 262144 | tf_op jit(solution)/shard_map/all_to_all | solution.py:163
  123.8 8.4 %all_to_all.26 = f32[1,2,8,4,256]{4,3,1,0,2:T(4,128)S(1)} all-to-all(f32[1,2,8,4,256]{4,3,1,0,2:T(4,128)S(1)} %copy.203), channel_id=1, replica_groups=mesh['gx'=8,'gy'=4] {'gx'}, dimensions={2} | all-to-all | bytes 131072 | tf_op jit(solution)/shard_map/all_to_all | solution.py:165
  (207 shorter events, 49.3 us)
Async XLA Ops:
  0.6 18.7 %copy-start.4 = (bf16[9,64,2]{1,2,0:T(2,128)(2,1)S(1)}, bf16[9,64,2]{1,2,0:T(2,128)(2,1)}, u32[]{:S(2)}) copy-start(bf16[9,64,2]{1,2,0:T(2,128)(2,1)} %param.13) | copy-start | bytes 6916
  0.6 18.7 %copy-start.5 = (f32[64]{0:T(128)S(1)}, f32[64]{0:T(128)}, u32[]{:S(2)}) copy-start(f32[64]{0:T(128)} %param.14) | copy-start | bytes 772
  0.7 18.7 %copy-start = (bf16[9,64,64]{2,1,0:T(8,128)(2,1)S(1)}, bf16[9,64,64]{2,1,0:T(8,128)(2,1)}, u32[]{:S(2)}) copy-start(bf16[9,64,64]{2,1,0:T(8,128)(2,1)} %param.15) | copy-start | bytes 221188
  0.7 18.7 %copy-start.6 = (f32[64]{0:T(128)S(1)}, f32[64]{0:T(128)}, u32[]{:S(2)}) copy-start(f32[64]{0:T(128)} %param.16) | copy-start | bytes 772
  0.7 18.7 %copy-start.3 = (bf16[9,16,64]{2,1,0:T(8,128)(2,1)S(1)}, bf16[9,16,64]{2,1,0:T(8,128)(2,1)}, u32[]{:S(2)}) copy-start(bf16[9,16,64]{2,1,0:T(8,128)(2,1)} %param.17) | copy-start | bytes 55300
  0.7 18.7 %copy-start.7 = (f32[16]{0:T(128)S(1)}, f32[16]{0:T(128)}, u32[]{:S(2)}) copy-start(f32[16]{0:T(128)} %param.18) | copy-start | bytes 196
  1.5 5.9 %collective-permute-start = (f32[2,3,256]{2,1,0:T(4,128)S(1)}, f32[2,3,256]{2,1,0:T(4,128)S(1)}, u32[]{:S(2)}, u32[]{:S(2)}) collective-permute-start(f32[2,3,256]{2,1,0:T(4,128)S(1)} %get-tuple-element.348), channel_id=1, source_target_pairs={{4,0},{8,4},{12,8},{16,12},{20,16},{24,20},{28,24},{0,28},{5,1},{9... | collective-permute-start | bytes 18440 | tf_op jit(solution)/shard_map/ppermute | solution.py:22
  6.0 4.9 %collective-permute-start.1 = (f32[2,3,256]{2,1,0:T(4,128)S(1)}, f32[2,3,256]{2,1,0:T(4,128)S(1)}, u32[]{:S(2)}, u32[]{:S(2)}) collective-permute-start(f32[2,3,256]{2,1,0:T(4,128)S(1)} %get-tuple-element.347), channel_id=1, source_target_pairs={{0,4},{4,8},{8,12},{12,16},{16,20},{20,24},{24,28},{28,0},{1,5},{5... | collective-permute-start | bytes 18440 | tf_op jit(solution)/shard_map/ppermute | solution.py:21
  11.8 4.8 %collective-permute-start.3 = (f32[2,38,3]{2,1,0:T(8,128)S(1)}, f32[2,38,3]{2,1,0:T(8,128)S(1)}, u32[]{:S(2)}, u32[]{:S(2)}) collective-permute-start(f32[2,38,3]{2,1,0:T(8,128)S(1)} %get-tuple-element.344), channel_id=1, source_target_pairs={{1,0},{2,1},{3,2},{0,3},{5,4},{6,5},{7,6},{4,7},{9,8},{10,9},{11,1... | collective-permute-start | bytes 2744 | tf_op jit(solution)/shard_map/ppermute | solution.py:22
  14.2 4.9 %collective-permute-start.2 = (f32[2,38,3]{2,1,0:T(8,128)S(1)}, f32[2,38,3]{2,1,0:T(8,128)S(1)}, u32[]{:S(2)}, u32[]{:S(2)}) collective-permute-start(f32[2,38,3]{2,1,0:T(8,128)S(1)} %get-tuple-element.343), channel_id=1, source_target_pairs={{0,1},{1,2},{2,3},{3,0},{4,5},{5,6},{6,7},{7,4},{8,9},{9,10},{10,1... | collective-permute-start | bytes 2744 | tf_op jit(solution)/shard_map/ppermute | solution.py:21
  19.4 34.7 %copy-start.8 = (f32[4]{0:T(128)S(1)}, f32[4]{0:T(128)}, u32[]{:S(2)}) copy-start(f32[4]{0:T(128)} %constant.257.clone) | copy-start | bytes 52
  54.0 0.8 copy-start.1
  54.0 0.8 copy-start.2
  54.9 5.2 %collective-permute-start.4 = (f32[2,1,256]{2,1,0:T(1,128)S(1)}, f32[2,1,256]{2,1,0:T(1,128)S(1)}, u32[]{:S(2)}, u32[]{:S(2)}) collective-permute-start(f32[2,1,256]{2,1,0:T(1,128)S(1)} %slice.909), channel_id=1, source_target_pairs={{28,0},{0,4},{4,8},{8,12},{12,16},{16,20},{20,24},{24,28},{29,1},{... | collective-permute-start | bytes 6152 | tf_op jit(solution)/shard_map/ppermute | solution.py:30
  55.3 4.8 %collective-permute-start.5 = (f32[2,32,1]{2,1,0:T(8,128)S(1)}, f32[2,32,1]{2,1,0:T(8,128)S(1)}, u32[]{:S(2)}, u32[]{:S(2)}) collective-permute-start(f32[2,32,1]{2,1,0:T(8,128)S(1)} %slice.917), channel_id=1, source_target_pairs={{3,0},{0,1},{1,2},{2,3},{7,4},{4,5},{5,6},{6,7},{11,8},{8,9},{9,10... | collective-permute-start | bytes 776 | tf_op jit(solution)/shard_map/ppermute | solution.py:30
  60.9 9.6 %all-to-all-start = ((f32[1,2,1,32,256]{4,1,2,0,3:T(2,128)}), f32[1,2,1,32,256]{4,1,2,0,3:T(2,128)S(1)}, u32[]{:S(2)}, u32[]{:S(2)}) async-start(f32[1,2,1,32,256]{4,1,2,0,3:T(2,128)} %copy.170), calls=%async_computation | async-start | bytes 131072 | tf_op jit(solution)/shard_map/all_to_all | solution.py:163
  71.7 10.1 %all-to-all-start.1 = ((f32[2,2,8,4,256]{4,3,1,0,2:T(4,128)}), f32[2,2,8,4,256]{4,3,1,0,2:T(4,128)S(1)}, u32[]{:S(2)}, u32[]{:S(2)}) async-start(f32[2,2,8,4,256]{4,3,1,0,2:T(4,128)} %copy.173), calls=%async_computation.1 | async-start | bytes 262144 | tf_op jit(solution)/shard_map/all_to_all | solution.py:165
  83.7 8.3 %all-to-all-start.2 = ((f32[2,2,1,32,256]{4,1,0,2,3:T(2,128)}), f32[2,2,1,32,256]{4,1,0,2,3:T(2,128)S(1)}, u32[]{:S(2)}, u32[]{:S(2)}) async-start(f32[2,2,1,32,256]{4,1,0,2,3:T(2,128)} %copy.180), calls=%async_computation.2 | async-start | bytes 262144 | tf_op jit(solution)/shard_map/all_to_all | solution.py:193
where the time goes:
time: 134 us
  matrix products  49.8 us (37%)
  waiting for transfers between devices  29.3 us (22%)
  blocking collectives  25 us (19%)
  starting transfers between devices  17.5 us (13%)
  other arithmetic  5.19 us (4%)
  local copies, waits for them, and re-layouts  4.84 us (4%)
    dot_general x108, matrix products, convolve(): jnp.einsum('oc,chw->ohw', kernel[tap_index], window, preferred_element_ty...  33.6 us
    dot_general x28, matrix products, product(): return jnp.einsum(form, matrix, values, precision=highest)  16.2 us
    all_to_all x1, blocking collectives, row_section(): lax.all_to_all(shaped, 'gx', split_axis=3, concat_axis=2, tiled=True)  9.23 us
    all_to_all x1, blocking collectives, row_section(): lax.all_to_all(turned, 'gx', split_axis=2, concat_axis=3, tiled=True)  8.4 us
    all_to_all x1, blocking collectives, column_home(): lax.all_to_all(spectra, 'gy', split_axis=2, concat_axis=3, tiled=True)  7.41 us
    ppermute x2, starting transfers between devices, padded_2(): after = lax.ppermute(first, axis, down)  6.94 us
    all_to_all x1, waiting for transfers between devices, row_section(): lax.all_to_all(turned, 'gx', split_axis=2, concat_axis=3, tiled=True)  6.62 us
    ppermute x2, waiting for transfers between devices, padded_2(): before = lax.ppermute(last, axis, up)  6.04 us
  transfers between devices with their start and end apart: 9, of which 7 were waited for; matrix products, arithmetic and copies ran while one was open for 2% of the time, Pallas kernels for 0%

commit v1 on v0

v1 whole, which is shorter than its diff:
```python
import functools
import math

import jax
import jax.numpy as jnp
import ml_dtypes
import numpy as np
from jax import lax
from jax.experimental import pallas as pl
from jax.experimental.pallas import tpu as pltpu
from jax.sharding import PartitionSpec as P

step_ratio = 0.4
stencil_base = (-0.0625, 0.5625, 0.5625, -0.0625)
f32 = jnp.float32
bf16 = jnp.bfloat16

vmem_limit = 48 * 1024 * 1024


def split(value):
    high = value.astype(bf16)
    return high, (value - high.astype(f32)).astype(bf16)


def split_table(table):
    high = table.astype(ml_dtypes.bfloat16)
    low = (table - high.astype(np.float64)).astype(ml_dtypes.bfloat16)
    return high, low


def dot(a, b):
    return jnp.dot(a, b, preferred_element_type=f32)


def product_3(value, high, low):
    rows = value.shape[0]
    first, second = split(value)
    both = dot(jnp.concatenate([first, second], axis=0), high)
    return both[:rows] + both[rows:] + dot(first, low)


def parity(shape):
    rows = lax.broadcasted_iota(jnp.int32, shape, 0)
    return jnp.where(rows % 8 < 4, 1.0, -1.0).astype(f32)


def swap(value):
    rows = value.shape[0]
    lower = lax.broadcasted_iota(jnp.int32, value.shape, 0) % 8 < 4
    return jnp.where(lower, pltpu.roll(value, rows - 4, 0), pltpu.roll(value, 4, 0))


def advance_kernel(
    u_ref, v_ref, bot_ref, top_ref, right_ref, left_ref, w1_ref, w2_ref, w3e_ref, w3o_ref,
    b1_ref, b2_ref, b3_ref, star_ref, field, first, second, coeff,
):
    height, breadth = u_ref.shape
    rows = height + 8
    groups = rows // 4
    lanes = breadth + 128
    field[:, :, breadth:] = jnp.zeros((2, rows + 16, 128), f32)
    for q, ref in enumerate((u_ref, v_ref)):
        field[q, 8 : 8 + height, :breadth] = ref[...]
        field[q, 8 + height : 12 + height, :breadth] = bot_ref[q]
        field[q, 12 + height : 16 + height, :breadth] = top_ref[q]
        field[q, 8 : 8 + rows, breadth : breadth + 4] = right_ref[q]
        field[q, 8 : 8 + rows, lanes - 4 : lanes] = left_ref[q]
        field[q, 0:8, :] = field[q, rows : rows + 8, :]
        field[q, 8 + rows : 16 + rows, :] = field[q, 8:16, :]
    whole = jnp.concatenate([field[0, 8 : 8 + rows], field[1, 8 : 8 + rows]], axis=0)
    pieces = [pltpu.roll(whole, 1, 1), whole, pltpu.roll(whole, lanes - 1, 1)]
    depth = w1_ref.shape[1]
    pieces.append(jnp.zeros((depth - 6 * rows, lanes), f32))
    turned = jnp.concatenate(pieces, axis=0).T
    patches = jnp.concatenate([turned[: breadth + 8], turned[lanes - 8 :]], axis=0).astype(bf16)
    span = breadth + 16
    for r in range(groups):
        first[r] = jnp.maximum(dot(patches, w1_ref[r]) + b1_ref[...], 0.0).astype(bf16)

    def gathered(source, r):
        before, after = (r - 1) % groups, (r + 1) % groups
        beside = jnp.concatenate([source[before, :, 128:], source[after, :, :128]], axis=1)
        return source[r], beside

    for r in range(groups):
        own, beside = gathered(first, r)
        total = dot(own, w2_ref[:256]) + dot(beside, w2_ref[256:])
        total = pltpu.roll(total[:, :256], 1, 0) + total[:, 256:512] + pltpu.roll(total[:, 512:], span - 1, 0)
        second[r] = jnp.maximum(total + b2_ref[...], 0.0).astype(bf16)

    def last(r, ref):
        own, beside = gathered(second, r)
        total = dot(own, ref[:256]) + dot(beside, ref[256:])
        left_part = total[:, :128]
        return pltpu.roll(left_part, 1, 0) + pltpu.roll(left_part, 64, 1) + pltpu.roll(total[:, 128:], span - 1, 0)

    def keep(r, block):
        coeff[r, :, :breadth] = block[:, :breadth]
        coeff[r, :, breadth:] = block[:, breadth:]

    pairs = [(i, i + 1) for i in range(0, groups - 2, 2)] + [(groups - 1, None)]
    for even, odd in pairs:
        block = last(even, w3e_ref)
        if odd is not None:
            other = last(odd, w3o_ref)
            lower = lax.broadcasted_iota(jnp.int32, block.shape, 1) < 64
            block = jnp.where(lower, block, other)
        block = jnp.concatenate(
            [block[: breadth + 8], jnp.zeros((lanes - span, 128), f32), block[breadth + 8 :]], axis=0
        ).T
        keep(even, block[:64])
        if odd is not None:
            keep(odd, block[64:])

    offsets = b3_ref[...]
    sub = lax.broadcasted_iota(jnp.int32, (8, breadth), 0) % 4

    def stacked(r, shift, qs=(0, 1)):
        start = 8 + 4 * r + shift
        return jnp.concatenate([field[q, start : start + 4, :] for q in qs], axis=0)

    previous = None
    for r in [groups - 1] + list(range(groups - 2)):
        weights = coeff[r] + offsets
        weights = [weights[8 * i : 8 * i + 8] for i in range(8)]
        centre = stacked(r, 0)

        def stencil(d):
            four = weights[4 * d : 4 * d + 4]
            mean = (four[0] + four[1] + four[2] + four[3]) * 0.25
            return [base + w - mean for base, w in zip(stencil_base, four)]

        east = stencil(0)
        flow_x = (
            east[0] * stacked(r, -1) + east[1] * centre + east[2] * stacked(r, 1) + east[3] * stacked(r, 2)
        )
        flow_x = flow_x * (0.5 * (stacked(r, 0, (0, 0)) + stacked(r, 1, (0, 0))))
        flow_x = flow_x[:, :breadth]
        if previous is not None:
            north = stencil(1)
            flow_y = (
                north[0] * pltpu.roll(centre, 1, 1)
                + north[1] * centre
                + north[2] * pltpu.roll(centre, lanes - 1, 1)
                + north[3] * pltpu.roll(centre, lanes - 2, 1)
            )
            carrier = stacked(r, 0, (1, 1))
            flow_y = flow_y * (0.5 * (carrier + pltpu.roll(carrier, lanes - 1, 1)))
            change_y = (flow_y - pltpu.roll(flow_y, 1, 1))[:, :breadth]
            above = jnp.where(sub == 0, pltpu.roll(previous, 5, 0), pltpu.roll(flow_x, 1, 0))
            star_ref[8 * r : 8 * r + 8, :] = centre[:, :breadth] - step_ratio * (flow_x - above + change_y)
        previous = flow_x


def column_kernel(blocks_ref, cos_ref, sin_ref, high_ref, low_ref, out_ref):
    count, rows, breadth = blocks_ref.shape
    sign = parity((rows, breadth))
    mixed = None
    for b in range(count):
        block = blocks_ref[b] * sign
        term = block * cos_ref[b : b + 1, :] + swap(block) * (sign * sin_ref[b : b + 1, :])
        mixed = term if mixed is None else mixed + term
    spectra = product_3(mixed, high_ref[...], low_ref[...])
    out_ref[...] = spectra[:, :breadth] + sign * swap(spectra[:, breadth:])


def row_kernel(
    gathered_ref, fwd_ref, fwd_low_ref, inv_ref, inv_low_ref, high_ref, low_ref, wave_ref, out_ref, *, scale
):
    length = gathered_ref.shape[0] // 2
    breadth = gathered_ref.shape[1]
    data, data_low = split(gathered_ref[...])
    spectra = dot(fwd_ref[...], data) + dot(fwd_ref[...], data_low) + dot(fwd_low_ref[...], data)
    real_part, imag_part = spectra[:length], spectra[length:]
    index = lax.broadcasted_iota(jnp.int32, (length, breadth), 0)
    wave_x = jnp.where(index >= length // 2, index - length, index).astype(f32) * (2.0 * math.pi / length)
    wave_y = wave_ref[0:1, :]
    edge_y = wave_ref[1:2, :] > 0.5
    edge_x = index == length // 2
    total = wave_x * wave_x + wave_y * wave_y
    zero = total == 0.0
    inverse = scale / jnp.where(zero, 1.0, total)
    same = (0.5 * inverse) * (wave_y * wave_y - wave_x * wave_x)
    cross = jnp.where(edge_x != edge_y, 0.0, -inverse * wave_x * wave_y)
    same_real = jnp.where(zero, 0.5 * scale, same)
    same_imag = jnp.where(zero, -0.5 * scale, same)
    kept_real = same_real * real_part - cross * imag_part
    kept_imag = same_imag * imag_part + cross * real_part
    kept, kept_low = split(jnp.concatenate([kept_real, kept_imag], axis=0))
    home = dot(inv_ref[...], kept) + dot(inv_ref[...], kept_low) + dot(inv_low_ref[...], kept)
    columns = product_3(home, high_ref[...], low_ref[...])
    rows = home.shape[0]
    out_ref[...] = columns[:, :breadth] - parity((rows, breadth)) * swap(columns[:, breadth:])


def home_kernel(blocks_ref, cos_ref, sin_ref, star_ref, u_ref, v_ref):
    count, rows, breadth = blocks_ref.shape
    sign = parity((rows, breadth))
    result = 0.5 * star_ref[...]
    for b in range(count):
        block = blocks_ref[b]
        result = result + block * cos_ref[b : b + 1, :] - swap(block) * (sign * sin_ref[b : b + 1, :])
    for r in range(rows // 8):
        u_ref[4 * r : 4 * r + 4, :] = result[8 * r : 8 * r + 4]
        v_ref[4 * r : 4 * r + 4, :] = result[8 * r + 4 : 8 * r + 8]


def call(kernel, shapes, scratch=(), flops=10**7):
    return pl.pallas_call(
        kernel,
        out_shape=shapes,
        scratch_shapes=list(scratch),
        compiler_params=pltpu.CompilerParams(vmem_limit_bytes=vmem_limit),
        cost_estimate=pl.CostEstimate(flops=flops, bytes_accessed=2**20, transcendentals=0),
    )


@functools.lru_cache(None)
def tables(height, breadth, members_x, members_y):
    turn = 2.0 * math.pi
    j = np.arange(breadth)
    phase = turn * (np.outer(j, j) % breadth) / breadth
    column = split_table(np.concatenate([np.cos(phase), np.sin(phase)], axis=1))
    length = height * members_x
    k = np.arange(length)
    phase = turn * (np.outer(k, k) % length) / length
    cosine = np.cos(phase).reshape(length, length // 4, 1, 4)
    sine = np.sin(phase).reshape(length, length // 4, 1, 4)
    real_rows = np.concatenate([cosine, sine], axis=2).reshape(length, 2 * length)
    imag_rows = np.concatenate([-sine, cosine], axis=2).reshape(length, 2 * length)
    forward = np.concatenate([real_rows, imag_rows], axis=0)
    forward_pair = split_table(forward)
    backward_pair = split_table(np.ascontiguousarray(forward.T))
    g = np.arange(members_y)
    count = np.multiply.outer(np.outer(g, g) * breadth, np.ones(breadth, np.int64)) + np.outer(
        np.ones(members_y, np.int64), j
    )[None] * g[None, :, None]
    phase = turn * (count % (breadth * members_y)) / (breadth * members_y)
    twiddle = np.stack([np.cos(phase), np.sin(phase)]).astype(np.float32)
    return column, forward_pair, backward_pair, twiddle


def own_part(table, index):
    return lax.dynamic_index_in_dim(jnp.asarray(table), index, 0, keepdims=False)


def stacked_weights(w_first, w_second, w_third, rows):
    groups = rows // 4
    taps_1 = w_first.astype(f32).reshape(3, 3, 64, 2).transpose(0, 1, 3, 2)
    wide = jnp.concatenate([taps_1] * 4, axis=-1).reshape(3, 6, 1, 256)
    wide = jnp.broadcast_to(wide, (3, 6, rows, 256)).reshape(3, 6 * rows, 256)
    depth = -(-6 * rows // 128) * 128
    wide = jnp.pad(wide, ((0, 0), (0, depth - 6 * rows), (0, 0)))
    place = (
        lax.broadcasted_iota(jnp.int32, (depth, 256), 0) % rows
        - lax.broadcasted_iota(jnp.int32, (depth, 256), 1) // 64
        + rows
    )
    group = jnp.arange(groups, dtype=jnp.int32)[:, None, None]
    kernel_1 = sum(
        jnp.where((place[None] - 4 * group + 2 * rows - d + 1) % rows == 0, wide[d][None], 0.0) for d in range(3)
    ).astype(bf16)
    choose = np.zeros((3, 8, 4), np.float32)
    for t in range(4):
        for d in range(3):
            source = t + d - 1
            slot = 5 if source < 0 else 6 if source > 3 else source
            choose[d, slot, t] = 1.0
    choose = jnp.asarray(choose, bf16)
    taps_2 = w_second.reshape(3, 3, 64, 64)
    kernel_2 = jnp.einsum("dkt,dcoi->kicto", choose, taps_2, preferred_element_type=f32)
    kernel_2 = kernel_2.astype(bf16).reshape(512, 768)
    order = np.array([8 * d + 4 * q + s for d in range(2) for s in range(4) for q in range(2)])
    taps_3 = w_third.reshape(3, 3, 16, 64)[:, :, order]
    kernel_3 = jnp.einsum("dkt,dcoi->kicot", choose, taps_3, preferred_element_type=f32)
    kernel_3 = kernel_3.astype(bf16).reshape(512, 3, 64)
    blank = jnp.zeros((512, 64), bf16)
    even = jnp.concatenate([kernel_3[:, 0], kernel_3[:, 1], kernel_3[:, 2], blank], axis=1)
    odd = jnp.concatenate([kernel_3[:, 1], kernel_3[:, 0], blank, kernel_3[:, 2]], axis=1)
    return kernel_1, kernel_2, even, odd, order


def gather(block, axis):
    return lax.all_gather(block, axis, axis=0, tiled=False)


def on_device(u_field, v_field, w_first, b_first, w_second, b_second, w_third, b_third):
    height, breadth = u_field.shape
    members_x, members_y = lax.axis_size("gx"), lax.axis_size("gy")
    index_x, index_y = lax.axis_index("gx"), lax.axis_index("gy")
    grid_x, grid_y = height * members_x, breadth * members_y
    rows = height + 8

    def shifted(value, axis, distance):
        peers = lax.axis_size(axis)
        return lax.ppermute(value, axis, [(i, (i + distance) % peers) for i in range(peers)])

    top = shifted(jnp.stack([u_field[-4:], v_field[-4:]]), "gx", 1)
    bottom = shifted(jnp.stack([u_field[:4], v_field[:4]]), "gx", -1)

    def edge(part):
        centre = jnp.stack([part(u_field), part(v_field)])
        return jnp.concatenate([centre, part(bottom), part(top)], axis=1)

    left = shifted(edge(lambda a: a[..., -4:]), "gy", 1)
    right = shifted(edge(lambda a: a[..., :4]), "gy", -1)

    kernel_1, kernel_2, even, odd, order = stacked_weights(w_first, w_second, w_third, rows)
    bias_1 = jnp.tile(b_first, 4)[None]
    bias_2 = jnp.tile(b_second, 4)[None]
    bias_3 = jnp.repeat(b_third[order], 4)[:, None]
    groups = rows // 4
    span = breadth + 16
    block = jax.ShapeDtypeStruct((2 * height, breadth), f32)
    star = call(
        advance_kernel,
        block,
        (
            pltpu.VMEM((2, rows + 16, breadth + 128), f32),
            pltpu.VMEM((groups, span, 256), bf16),
            pltpu.VMEM((groups, span, 256), bf16),
            pltpu.VMEM((groups, 64, breadth + 128), f32),
        ),
        flops=10**9,
    )(u_field, v_field, bottom, top, right, left, kernel_1, kernel_2, even, odd, bias_1, bias_2, bias_3)

    column, forward, backward, twiddle = tables(height, breadth, members_x, members_y)
    cosine, sine = own_part(twiddle[0], index_y), own_part(twiddle[1], index_y)
    turned = twiddle.transpose(0, 2, 1, 3)
    cosine_out, sine_out = own_part(turned[0], index_y), own_part(turned[1], index_y)
    column = [jnp.asarray(t) for t in column]
    spectra = call(column_kernel, block)(gather(star, "gy"), cosine_out, sine_out, *column)
    number_y = index_y + members_y * jnp.arange(breadth, dtype=jnp.int32)
    wave_y = jnp.where(number_y >= grid_y // 2, number_y - grid_y, number_y).astype(f32) * (2.0 * math.pi / grid_y)
    wave = jnp.stack([wave_y, (number_y == grid_y // 2).astype(f32)])
    back = [
        lax.dynamic_slice_in_dim(jnp.asarray(t), index_x * 2 * height, 2 * height, axis=0) for t in backward
    ]
    everything = gather(spectra, "gx").reshape(2 * grid_x, breadth)
    columns = call(functools.partial(row_kernel, scale=1.0 / (grid_x * grid_y)), block)(
        everything, *[jnp.asarray(t) for t in forward], *back, *column, wave
    )
    part = jax.ShapeDtypeStruct((height, breadth), f32)
    return tuple(call(home_kernel, (part, part))(gather(columns, "gy"), cosine, sine, star))


def solution(mesh):
    return jax.shard_map(
        on_device,
        mesh=mesh,
        in_specs=(P("gx", "gy"), P("gx", "gy"), P(), P(), P(), P(), P(), P()),
        out_specs=(P("gx", "gy"), P("gx", "gy")),
        check_vma=False,
    )
```

time: 134 us -> 72.9 us (0.54)
  matrix products: 49.8 us -> 2.3 us
  waiting for transfers between devices: 29.3 us -> 0.01 us
  starting transfers between devices: 17.5 us -> 7.1 us
  local copies, waits for them, and re-layouts: 4.84 us -> 14.7 us
  blocking collectives: 25 us -> 33.4 us
  Pallas kernels: 0 us -> 6.9 us
  other arithmetic: 5.19 us -> 6.9 us
    dot_general x136 -> x2, matrix products: 49.8 us -> 2.3 us  [the longest x1 2 us: stacked_weights(): jnp.einsum('dkt,dcoi->kicto', choose, taps_2, preferred_element_type=f32)]
    all_gather x0 -> x3, blocking collectives: none -> 33.4 us  [gather(): return lax.all_gather(block, axis, axis=0, tiled=False)]
    all_to_all x3 -> x0, blocking collectives: 25 us -> none  [the longest x1 9.23 us: row_section(): lax.all_to_all(shaped, 'gx', split_axis=3, concat_axis=2, tiled=True)]
    all_to_all x3 -> x0, waiting for transfers between devices: 17.1 us -> none  [the longest x1 6.62 us: row_section(): lax.all_to_all(turned, 'gx', split_axis=2, concat_axis=3, tiled=True)]
    ppermute x6 -> x4, waiting for transfers between devices: 12.2 us -> 0.01 us  [shifted(): lax.ppermute(value, axis, [(i, (i + distance) % peers) for i in range(pee...]
    all_to_all x3 -> x0, starting transfers between devices: 10.5 us -> none  [the longest x1 3.65 us: row_section(): lax.all_to_all(shaped, 'gx', split_axis=3, concat_axis=2, tiled=True)]
    pallas_call x0 -> x4, Pallas kernels: none -> 6.9 us  [the longest x1 4.56 us: on_device(): call(advance_kernel, block, (pltpu.VMEM((2, rows + 16, breadth + 128), f3...]
    convert_element_type x0 -> x2, other arithmetic: none -> 5.33 us  [the longest x1 5.32 us: stacked_weights(): kernel_1 = sum((jnp.where((place[None] - 4 * group + 2 * rows - d + 1) %...]
  transfers between devices with their start and end apart: 9 -> 4, of which waited for: 7 -> 0; matrix products, arithmetic and copies ran while one was open for 2% -> 32% of each run, Pallas kernels for 0% -> 0%
where the time goes in v1:
time: 72.9 us; the launch traced here: 72.3 us
  blocking collectives  33.4 us (46%)
  local copies, waits for them, and re-layouts  14.7 us (20%)
  starting transfers between devices  7.1 us (10%)
  other arithmetic  6.9 us (9%)
  Pallas kernels  6.9 us (9%)
  matrix products  2.3 us (3%)
  between operations  1.03 us (1%)
    all_gather x3, blocking collectives, gather(): return lax.all_gather(block, axis, axis=0, tiled=False)  33.4 us
    ppermute x4, starting transfers between devices, shifted(): lax.ppermute(value, axis, [(i, (i + distance) % peers) for i in range(pee...  7.1 us
    convert_element_type x1, other arithmetic, stacked_weights(): kernel_1 = sum((jnp.where((place[None] - 4 * group + 2 * rows - d + 1) %...  5.32 us
    pallas_call x1, Pallas kernels, on_device(): call(advance_kernel, block, (pltpu.VMEM((2, rows + 16, breadth + 128), f3...  4.56 us
    convert_element_type x1, local copies, waits for them, and re-layouts, stacked_weights(): kernel_2 = kernel_2.astype(bf16).reshape(512, 768)  4.03 us
    reshape x1, local copies, waits for them, and re-layouts, stacked_weights(): kernel_2 = kernel_2.astype(bf16).reshape(512, 768)  2.88 us
    dot_general x1, matrix products, stacked_weights(): jnp.einsum('dkt,dcoi->kicto', choose, taps_2, preferred_element_type=f32)  2 us
    slice x6, local copies, waits for them, and re-layouts, on_device(): left = shifted(edge(lambda a: a[..., -4:]), 'gy', 1)  1.91 us
  transfers between devices with their start and end apart: 4, of which 0 were waited for; matrix products, arithmetic and copies ran while one was open for 32% of the time, Pallas kernels for 0%

profile of v1, /device:TPU:0, one launch (start us, length us, event | category | flops | bytes accessed | tf_op | source)
XLA Modules:
  0.0 72.3 jit_solution(16799990195612346499)
XLA Ops:
  0.7 0.8 %slice_bitcast_fusion = (f32[1,4,256]{2,1,0:T(4,128)S(1)}, f32[1,4,256]{2,1,0:T(4,128)S(1)}, f32[1,4,256]{2,1,0:T(4,128)S(1)}, f32[1,4,256]{2,1,0:T(4,128)S(1)}) fusion(f32[32,256]{1,0:T(8,128)} %v_ref.1, f32[32,256]{1,0:T(8,128)} %u_ref.1), kind=kLoop, calls=%fused_computation.53 | loop fusion | bytes 32768 | tf_op jit(solution)/shard_map/stack | solution.py:299
  1.5 4.5 %collective-permute-start = (f32[2,4,256]{2,1,0:T(4,128)S(1)}, f32[2,4,256]{2,1,0:T(4,128)S(1)}, u32[]{:S(2)}, u32[]{:S(2)}) collective-permute-start(f32[2,4,256]{2,1,0:T(4,128)S(1)} %pad_maximum_fusion.4), channel_id=1, source_target_pairs={{0,28},{4,0},{8,4},{12,8},{16,12},{20,16},{24,20},{28,24},{1,29},{... | collective-permute-start | bytes 24584 | tf_op jit(solution)/shard_map/ppermute | solution.py:297
  6.0 0.8 %fusion.28 = (f32[32,4]{1,0:T(8,128)S(1)}, f32[32,4]{1,0:T(8,128)S(1)}) fusion(f32[32,256]{1,0:T(8,128)} %v_ref.1), kind=kLoop, calls=%fused_computation.75 | loop fusion | bytes 2048 | tf_op jit(solution)/shard_map/slice | solution.py:306
  6.8 0.8 %fusion.27 = (f32[32,4]{1,0:T(8,128)S(1)}, f32[32,4]{1,0:T(8,128)S(1)}) fusion(f32[32,256]{1,0:T(8,128)} %u_ref.1), kind=kLoop, calls=%fused_computation.74 | loop fusion | bytes 2048 | tf_op jit(solution)/shard_map/slice | solution.py:306
  8.0 0.9 %maximum_convert_fusion = f32[3,3,2,256]{3,2,1,0:T(2,128)S(1)} fusion(bf16[3,3,2,64]{3,2,1,0:T(2,128)(2,1)} %bitcast.71), kind=kLoop, calls=%fused_computation.42 | loop fusion | flops 36864 | bytes 20736 | tf_op jit(solution)/shard_map/broadcast_in_dim | solution.py:252
  9.2 0.6 gather_fusion
  9.8 0.3 fusion.16
  10.8 2.0 %fusion.15 = bf16[8,64,3,4,64]{1,0,4,2,3:T(8,128)(2,1)} fusion(bf16[3,8,4,1,1]{1,0,4,3,2:T(4,128)(2,1)S(1)} %copy-done.9, bf16[3,3,64,64]{3,2,1,0:T(8,128)(2,1)S(1)} %bitcast.64), kind=kOutput, calls=%fused_computation.25 | convolution fusion | flops 2752512 | bytes 860352 | tf_op jit(solution)/shard_map/dkt,dcoi->kicto/dot_general | solution.py:272
  12.8 0.7 dynamic-slice_bitcast_fusion.2
  13.5 0.7 dynamic-slice_bitcast_fusion
  14.2 0.9 %constant_dynamic-slice_fusion = (bf16[64,512]{1,0:T(8,128)(2,1)S(1)}, bf16[64,512]{1,0:T(8,128)(2,1)S(1)}) fusion(bf16[512,512]{1,0:T(8,128)(2,1)} %constant.136.clone, s32[]{:T(128)S(6)} %select_n.91, bf16[512,512]{1,0:T(8,128)(2,1)} %constant.135.clone), kind=kLoop, calls=%fused_computation.64 | loop fusion | bytes 262148 | tf_op jit(solution)/shard_map/dynamic_slice | solution.py:338
  15.2 0.4 pad_maximum_fusion.1
  15.7 5.3 %add_convert_fusion.w1_ref = bf16[10,256,256]{2,1,0:T(8,128)(2,1)S(1)} fusion(f32[256,256]{1,0:T(8,128)S(1)} %get-tuple-element.4, f32[256,256]{1,0:T(8,128)S(1)} %get-tuple-element.3, f32[256,256]{1,0:T(8,128)S(1)} %get-tuple-element.2, s32[10]{0:T(128)S(1)} %iota_multiply_fusion, s32[256,256]{1,0:T(8,128)S(1)} %subtract_add_fusion.3), kind=kLoop, calls=%fused_computation.20 | loop fusion | flops 20316160 | bytes 2359336 | tf_op jit(solution)/shard_map/convert_element_type | solution.py:263
  21.4 2.5 %collective-permute-start.2 = (f32[2,40,4]{2,1,0:T(8,128)S(1)}, f32[2,40,4]{2,1,0:T(8,128)S(1)}, u32[]{:S(2)}, u32[]{:S(2)}) collective-permute-start(f32[2,40,4]{2,1,0:T(8,128)S(1)} %pad_maximum_fusion.2), channel_id=1, source_target_pairs={{0,3},{1,0},{2,1},{3,2},{4,7},{5,4},{6,5},{7,6},{8,11},{9,8},{10,9... | collective-permute-start | bytes 3848 | tf_op jit(solution)/shard_map/ppermute | solution.py:297
  24.0 4.0 %copy.92 = bf16[8,64,3,4,64]{4,3,2,1,0:T(4,128)(2,1)} copy(bf16[8,64,3,4,64]{1,0,4,2,3:T(8,128)(2,1)} %fusion.15) | data formatting | bytes 1572864 | tf_op jit(solution)/shard_map/convert_element_type | solution.py:273
  28.0 2.9 %reshape.149.w2_ref = bf16[512,768]{1,0:T(8,128)(2,1)S(1)} reshape(bf16[8,64,3,4,64]{4,3,2,1,0:T(4,128)(2,1)} %copy.92) | data formatting | bytes 1572864 | tf_op jit(solution)/shard_map/reshape | solution.py:273
  31.1 0.7 gather_fusion.1
  32.0 4.6 %shard_map.221.star_ref = f32[64,256]{1,0:T(8,128)S(1)} custom-call(f32[32,256]{1,0:T(8,128)S(1)} %copy-done.5, f32[32,256]{1,0:T(8,128)S(1)} %copy-done.6, f32[2,4,256]{2,1,0:T(4,128)S(1)} %collective-permute-done.bot_ref, f32[2,4,256]{2,1,0:T(4,128)S(1)} %collective-permute-done.1.top_ref, f32[2,40,4]{2,1,0:T(8,128)S(1)} %collective-permute-done.2.right_ref, ...), custom_call_target="tpu_custom_call" | custom-call | flops 1000000000 | bytes 1048576 | tf_op jit(solution)/shard_map/pallas_call | solution.py:316
  36.6 9.9 %all-gather = f32[256,256]{1,0:T(8,128)S(1)} all-gather(f32[64,256]{1,0:T(8,128)S(1)} %shard_map.221.star_ref), channel_id=2, replica_groups=mesh['gx'=8,'gy'=4] {'gy'}, dimensions={0}, use_global_device_ids=true | all-gather | bytes 327680 | tf_op jit(solution)/shard_map/all_gather | solution.py:285
  46.5 0.3 shard_map.222
  46.8 14.8 %all-gather.1.gathered_ref = f32[512,256]{1,0:T(8,128)S(1)} all-gather(f32[64,256]{1,0:T(8,128)S(1)} %shard_map.222), channel_id=3, replica_groups=mesh['gx'=8,'gy'=4] {'gx'}, dimensions={0}, use_global_device_ids=true | all-gather | bytes 589824 | tf_op jit(solution)/shard_map/all_gather | solution.py:285
  61.6 1.4 %shard_map.223 = f32[64,256]{1,0:T(8,128)S(1)} custom-call(f32[512,256]{1,0:T(8,128)S(1)} %all-gather.1.gathered_ref, bf16[512,512]{1,0:T(8,128)(2,1)S(1)} %copy-done.3, bf16[512,512]{1,0:T(8,128)(2,1)S(1)} %copy-done.4, bf16[64,512]{1,0:T(8,128)(2,1)S(1)} %get-tuple-element.35.inv_ref, bf16[64,512]{1,0:T(8,128)(2,1)S(1)} %get-tuple-element.34.inv_low_ref, ...), custom_call_target="tpu_custom_call" | custom-call | flops 10000000 | bytes 1048576 | tf_op jit(solution)/shard_map/pallas_call | solution.py:341
  63.0 8.6 %all-gather.2 = f32[256,256]{1,0:T(8,128)S(1)} all-gather(f32[64,256]{1,0:T(8,128)S(1)} %shard_map.223), channel_id=4, replica_groups=mesh['gx'=8,'gy'=4] {'gy'}, dimensions={0}, use_global_device_ids=true | all-gather | bytes 327680 | tf_op jit(solution)/shard_map/all_gather | solution.py:285
  71.6 0.7 shard_map.224
  (73 shorter events, 2.2 us)
Async XLA Ops:
  0.6 30.5 %copy-start = (f32[16]{0:T(128)S(1)}, f32[16]{0:T(128)}, u32[]{:S(2)}) copy-start(f32[16]{0:T(128)} %param.29) | copy-start | bytes 196
  0.6 8.5 %copy-start.13 = (s32[16]{0:T(128)S(1)}, s32[16]{0:T(128)}, u32[]{:S(2)}) copy-start(s32[16]{0:T(128)} %constant.142) | copy-start | bytes 196
  0.7 9.1 %copy-start.10 = (bf16[3,8,4,1,1]{1,0,2,4,3:T(4,128)(2,1)S(1)}, bf16[3,8,4,1,1]{1,0,2,4,3:T(4,128)(2,1)}, u32[]{:S(2)}) copy-start(bf16[3,8,4,1,1]{1,0,2,4,3:T(4,128)(2,1)} %constant.145) | copy-start | bytes 580
  0.7 8.4 %copy-start.8 = (bf16[9,16,64]{2,1,0:T(8,128)(2,1)S(1)}, bf16[9,16,64]{2,1,0:T(8,128)(2,1)}, u32[]{:S(2)}) copy-start(bf16[9,16,64]{2,1,0:T(8,128)(2,1)} %param.28) | copy-start | bytes 55300
  1.5 19.8 %collective-permute-start = (f32[2,4,256]{2,1,0:T(4,128)S(1)}, f32[2,4,256]{2,1,0:T(4,128)S(1)}, u32[]{:S(2)}, u32[]{:S(2)}) collective-permute-start(f32[2,4,256]{2,1,0:T(4,128)S(1)} %pad_maximum_fusion.4), channel_id=1, source_target_pairs={{0,28},{4,0},{8,4},{12,8},{16,12},{20,16},{24,20},{28,24},{1,29},{... | collective-permute-start | bytes 24584 | tf_op jit(solution)/shard_map/ppermute | solution.py:297
  6.0 15.2 %collective-permute-start.1 = (f32[2,4,256]{2,1,0:T(4,128)S(1)}, f32[2,4,256]{2,1,0:T(4,128)S(1)}, u32[]{:S(2)}, u32[]{:S(2)}) collective-permute-start(f32[2,4,256]{2,1,0:T(4,128)S(1)} %pad_maximum_fusion.5), channel_id=1, source_target_pairs={{0,4},{4,8},{8,12},{12,16},{16,20},{20,24},{24,28},{28,0},{1,5},{5... | collective-permute-start | bytes 24584 | tf_op jit(solution)/shard_map/ppermute | solution.py:297
  9.0 1.8 %copy-start.7 = (bf16[9,64,64]{2,1,0:T(8,128)(2,1)S(1)}, bf16[9,64,64]{2,1,0:T(8,128)(2,1)}, u32[]{:S(2)}) copy-start(bf16[9,64,64]{2,1,0:T(8,128)(2,1)} %param.26) | copy-start | bytes 221188
  9.0 1.8 %copy-start.9 = (bf16[3,8,4,1,1]{1,0,4,3,2:T(4,128)(2,1)S(1)}, bf16[3,8,4,1,1]{1,0,4,3,2:T(4,128)(2,1)}, u32[]{:S(2)}) copy-start(bf16[3,8,4,1,1]{1,0,4,3,2:T(4,128)(2,1)} %constant.144) | copy-start | bytes 580
  21.4 10.5 %collective-permute-start.2 = (f32[2,40,4]{2,1,0:T(8,128)S(1)}, f32[2,40,4]{2,1,0:T(8,128)S(1)}, u32[]{:S(2)}, u32[]{:S(2)}) collective-permute-start(f32[2,40,4]{2,1,0:T(8,128)S(1)} %pad_maximum_fusion.2), channel_id=1, source_target_pairs={{0,3},{1,0},{2,1},{3,2},{4,7},{5,4},{6,5},{7,6},{8,11},{9,8},{10,9... | collective-permute-start | bytes 3848 | tf_op jit(solution)/shard_map/ppermute | solution.py:297
  23.9 8.0 %collective-permute-start.3 = (f32[2,40,4]{2,1,0:T(8,128)S(1)}, f32[2,40,4]{2,1,0:T(8,128)S(1)}, u32[]{:S(2)}, u32[]{:S(2)}) collective-permute-start(f32[2,40,4]{2,1,0:T(8,128)S(1)} %pad_maximum_fusion.3), channel_id=1, source_target_pairs={{0,1},{1,2},{2,3},{3,0},{4,5},{5,6},{6,7},{7,4},{8,9},{9,10},{10,1... | collective-permute-start | bytes 3848 | tf_op jit(solution)/shard_map/ppermute | solution.py:297
  28.0 2.9 %copy-start.11 = (f32[64]{0:T(128)S(1)}, f32[64]{0:T(128)}, u32[]{:S(2)}) copy-start(f32[64]{0:T(128)} %param.25) | copy-start | bytes 772
  28.0 3.0 %copy-start.12 = (f32[64]{0:T(128)S(1)}, f32[64]{0:T(128)}, u32[]{:S(2)}) copy-start(f32[64]{0:T(128)} %param.27) | copy-start | bytes 772
  28.0 3.9 %copy-start.5 = (f32[32,256]{1,0:T(8,128)S(1)}, f32[32,256]{1,0:T(8,128)}, u32[]{:S(2)}) copy-start(f32[32,256]{1,0:T(8,128)} %u_ref.1) | copy-start | bytes 98308
  28.0 3.9 %copy-start.6 = (f32[32,256]{1,0:T(8,128)S(1)}, f32[32,256]{1,0:T(8,128)}, u32[]{:S(2)}) copy-start(f32[32,256]{1,0:T(8,128)} %v_ref.1) | copy-start | bytes 98308
  32.0 14.5 %copy-start.1 = (bf16[256,512]{1,0:T(8,128)(2,1)S(1)}, bf16[256,512]{1,0:T(8,128)(2,1)}, u32[]{:S(2)}) copy-start(bf16[256,512]{1,0:T(8,128)(2,1)} %constant.133.clone.high_ref) | copy-start | bytes 786436
  32.0 14.5 %copy-start.2 = (bf16[256,512]{1,0:T(8,128)(2,1)S(1)}, bf16[256,512]{1,0:T(8,128)(2,1)}, u32[]{:S(2)}) copy-start(bf16[256,512]{1,0:T(8,128)(2,1)} %constant.134.clone.low_ref) | copy-start | bytes 786436
  36.5 25.1 %copy-start.3 = (bf16[512,512]{1,0:T(8,128)(2,1)S(1)}, bf16[512,512]{1,0:T(8,128)(2,1)}, u32[]{:S(2)}) copy-start(bf16[512,512]{1,0:T(8,128)(2,1)} %constant.137.clone.fwd_ref) | copy-start | bytes 1572868
  36.5 25.1 %copy-start.4 = (bf16[512,512]{1,0:T(8,128)(2,1)S(1)}, bf16[512,512]{1,0:T(8,128)(2,1)}, u32[]{:S(2)}) copy-start(bf16[512,512]{1,0:T(8,128)(2,1)} %constant.138.clone.fwd_low_ref) | copy-start | bytes 1572868
